TPU v7x, 256 devices: a whole 4x4x8 slice. The times are simulated.
256 devices in a mesh: row: 8 (over z), col: 32 (over y, x, core).
Axes of the slice: x: 4, y: 4, z: 8, core: 2. Of those that a mesh axis runs over, the one named last changes fastest.
Arguments:
- features: bfloat16 [131072, 128], P(('row', 'col')), may hold values from -6 to 6
- block_rows: int32 [8, 32, 64], P('row', 'col'), may hold values from 0 to 127
- block_cols: int32 [8, 32, 64], P('row', 'col'), may hold values from 0 to 31
- block_values: bfloat16 [8, 32, 64, 128, 128], P('row', 'col'), may hold values from -0.125 to 0.125
- weight_one: bfloat16 [128, 256], replicated, may hold values from -0.5 to 0.5
- bias_one: float32 [256], replicated, may hold values from -3 to 3
- weight_two: bfloat16 [256, 256], replicated, may hold values from -0.375 to 0.375
- bias_two: float32 [256], replicated, may hold values from -3 to 3
Outputs:
- hidden_two: bfloat16 [131072, 256], P(('row', 'col'))
All inputs are finite; a program needn't handle non-finite values.
Results may differ from a plain program's by a relative error of at most 0.0065.
Values may be sent and summed in bfloat16 or wider, within the bound.
A program may use at most 128 MiB of HBM per device.

v0:
```python
import jax
import jax.numpy as jnp
from jax import lax
from jax.sharding import PartitionSpec as P


def aggregate(node_feats, local_rows, local_cols, values):
    block = values.shape[1]
    width = node_feats.shape[1]
    own_rows = node_feats.shape[0]
    gathered = lax.all_gather(node_feats, "row", axis=0, tiled=True)
    blocks = gathered.reshape(gathered.shape[0] // block, block, width)
    tiles = blocks[local_cols]
    products = jnp.einsum("eij,ejf->eif", values, tiles, preferred_element_type=jnp.float32)
    groups = lax.axis_size("col")
    group_blocks = groups * (own_rows // block)
    partial_sum = jax.ops.segment_sum(products, local_rows, num_segments=group_blocks)
    flat_sum = partial_sum.reshape(group_blocks * block, width)
    mine = lax.psum_scatter(flat_sum, "col", scatter_dimension=0, tiled=True)
    return mine.astype(jnp.bfloat16)


def local(
    features, block_rows, block_cols, block_values, weight_one, bias_one, weight_two, bias_two
):
    local_rows = block_rows.reshape(-1)
    local_cols = block_cols.reshape(-1)
    values = block_values.reshape(local_rows.shape[0], block_values.shape[3], block_values.shape[4])
    agg_one = aggregate(features, local_rows, local_cols, values)
    hidden_one = jax.nn.relu(
        jnp.dot(agg_one, weight_one, preferred_element_type=jnp.float32) + bias_one
    ).astype(jnp.bfloat16)
    agg_two = aggregate(hidden_one, local_rows, local_cols, values)
    return jax.nn.relu(
        jnp.dot(agg_two, weight_two, preferred_element_type=jnp.float32) + bias_two
    ).astype(jnp.bfloat16)


def solution(mesh):
    placed = (
        P(("row", "col"), None),
        P("row", "col", None),
        P("row", "col", None),
        P("row", "col", None, None, None),
        P(),
        P(),
        P(),
        P(),
    )
    return jax.shard_map(
        local, mesh=mesh, in_specs=placed, out_specs=P(("row", "col"), None), check_vma=False
    )
```

profile of v0, /device:TPU:1, one launch (start us, length us, event | category | flops | bytes accessed | tf_op | source)
XLA Modules:
  0.0 402.0 jit_solution(10321986898646168197)
XLA Ops:
  6.5 0.0 copy-start
  6.5 0.0 all-gather.3.cloned.1.call-start
  6.5 0.7 all-gather.3.cloned.1.call-update
  7.3 0.0 reduce-scatter.3.cloned.1.call-start
  7.3 0.7 fusion.8
  8.0 38.6 %all-gather.3.cloned.1.call-done = bf16[4096,128]{1,0:T(8,128)(2,1)} async-done(((bf16[512,128]{1,0:T(8,128)(2,1)}), bf16[4096,128]{1,0:T(8,128)(2,1)}) %all-gather.3.cloned.1.call-update) | async-done | bytes 1048592 | tf_op jit(solution)/shard_map/all_gather | solution.py:11
  46.6 3.4 gather_fusion
  50.0 0.0 copy-done
  50.0 5.1 %convolution_bitcast_fusion.1 = f32[64,128,128]{1,2,0:T(8,128)} fusion(bf16[64,128,128]{2,1,0:T(8,128)(2,1)} %gather_fusion, bf16[1,1,64,128,128]{4,3,2,1,0:T(8,128)(2,1)S(1)} %copy-done), kind=kOutput, calls=%fused_computation.5 | convolution fusion | flops 268435456 | bytes 8388608 | tf_op jit(solution)/shard_map/eij,ejf->eif/dot_general | solution.py:14
  55.1 5.6 %copy.12 = f32[64,128,128]{2,1,0:T(8,128)} copy(f32[64,128,128]{1,2,0:T(8,128)} %convolution_bitcast_fusion.1) | data formatting | bytes 8388608 | tf_op jit(solution)/shard_map/eij,ejf->eif/dot_general | solution.py:14
  60.7 0.0 copy-start.3
  60.7 4.3 %broadcast_in_dim.5 = f32[128,128,128]{2,1,0:T(8,128)} broadcast(f32[]{:T(128)} %constant.3.clone.1), dimensions={} | broadcast | bytes 8388612 | tf_op jit(solution)/shard_map/broadcast_in_dim | solution.py:17
  65.0 0.0 copy-done.3
  65.0 13.7 %scatter_fusion = f32[128,128,128]{2,1,0:T(8,128)} fusion(f32[128,128,128]{2,1,0:T(8,128)} %broadcast_in_dim.5, s32[64]{0:T(128)S(1)} %bitcast.26, f32[64,128,128]{2,1,0:T(8,128)} %copy.12), kind=kCustom, calls=%fused_computation.2 | custom fusion | flops 1048576 | bytes 12583168 | tf_op jit(solution)/shard_map/scatter-add | solution.py:17
  78.8 0.0 copy-start.2
  78.8 0.0 copy-start.4
  78.8 0.0 reduce-scatter.3.cloned.1.call-update
  78.8 0.0 all-gather.5.cloned.1.call-start
  78.8 102.2 %reduce-scatter.3.cloned.1.call-done = f32[512,128]{1,0:T(8,128)} async-done(((f32[16384,128]{1,0:T(8,128)}), f32[512,128]{1,0:T(8,128)}) %reduce-scatter.3.cloned.1.call-update) | async-done | bytes 262160 | tf_op jit(solution)/shard_map/reduce_scatter | solution.py:19
  181.1 0.0 copy-done.2
  181.1 0.0 copy-done.4
  181.1 1.9 fusion.4
  182.9 0.0 all-gather.5.cloned.1.call-update
  183.0 0.0 reduce-scatter.5.cloned.1.call-start
  183.0 38.6 %all-gather.5.cloned.1.call-done = bf16[4096,256]{1,0:T(8,128)(2,1)} async-done(((bf16[512,256]{1,0:T(8,128)(2,1)}), bf16[4096,256]{1,0:T(8,128)(2,1)}) %all-gather.5.cloned.1.call-update) | async-done | bytes 2097168 | tf_op jit(solution)/shard_map/all_gather | solution.py:11
  221.6 4.4 %gather_fusion.1 = bf16[64,128,256]{2,1,0:T(8,128)(2,1)} fusion(bf16[32,128,256]{2,1,0:T(8,128)(2,1)} %bitcast.24, s32[1024]{0:T(1024)S(1)} %pad_clamp_fusion), kind=kCustom, calls=%fused_computation.1 | custom fusion | bytes 8388864 | tf_op jit(solution)/shard_map/gather | solution.py:13
  226.0 6.7 %convolution_bitcast_fusion = f32[64,128,256]{1,2,0:T(8,128)} fusion(bf16[64,128,256]{2,1,0:T(8,128)(2,1)} %gather_fusion.1, bf16[1,1,64,128,128]{4,3,2,1,0:T(8,128)(2,1)S(1)} %copy-done), kind=kOutput, calls=%fused_computation.4 | convolution fusion | flops 536870912 | bytes 14680064 | tf_op jit(solution)/shard_map/eij,ejf->eif/dot_general | solution.py:14
  232.7 9.0 %copy.14 = f32[64,128,256]{2,1,0:T(8,128)} copy(f32[64,128,256]{1,2,0:T(8,128)} %convolution_bitcast_fusion) | data formatting | bytes 16777216 | tf_op jit(solution)/shard_map/eij,ejf->eif/dot_general | solution.py:14
  241.7 7.8 %broadcast_in_dim.4 = f32[128,128,256]{2,1,0:T(8,128)} broadcast(f32[]{:T(128)} %constant.3.clone.1), dimensions={} | broadcast | bytes 16777220 | tf_op jit(solution)/shard_map/broadcast_in_dim | solution.py:17
  249.6 19.8 %scatter_fusion.1 = f32[128,128,256]{2,1,0:T(8,128)} fusion(f32[128,128,256]{2,1,0:T(8,128)} %broadcast_in_dim.4, s32[64]{0:T(128)S(1)} %bitcast.27, f32[64,128,256]{2,1,0:T(8,128)} %copy.14), kind=kCustom, calls=%fused_computation.3 | custom fusion | flops 2097152 | bytes 25166080 | tf_op jit(solution)/shard_map/scatter-add | solution.py:17
  269.4 0.0 copy-start.1
  269.4 0.0 copy-start.5
  269.4 0.0 reduce-scatter.5.cloned.1.call-update
  269.4 124.1 %reduce-scatter.5.cloned.1.call-done = f32[512,256]{1,0:T(8,128)} async-done(((f32[16384,256]{1,0:T(8,128)}), f32[512,256]{1,0:T(8,128)}) %reduce-scatter.5.cloned.1.call-update) | async-done | bytes 524304 | tf_op jit(solution)/shard_map/reduce_scatter | solution.py:19
  393.5 0.0 copy-done.1
  393.5 0.0 copy-done.5
  393.5 2.0 fusion.5
  (1 shorter events, 0.0 us)
Async XLA Ops:
  6.5 43.4 %copy-start = (bf16[1,1,64,128,128]{4,3,2,1,0:T(8,128)(2,1)S(1)}, bf16[1,1,64,128,128]{4,3,2,1,0:T(8,128)(2,1)}, u32[]{:S(2)}) copy-start(bf16[1,1,64,128,128]{4,3,2,1,0:T(8,128)(2,1)} %param.11) | copy-start | bytes 6291460
  6.5 40.1 %all-gather.3.cloned.1.call-start = ((), (), s32[]{:S(2)}) async-start(), calls=%async_computation.2 | async-start | bytes 1179648 | tf_op jit(solution)/shard_map/all_gather | solution.py:11
  7.3 173.8 %reduce-scatter.3.cloned.1.call-start = ((), (), s32[]{:S(2)}) async-start(), calls=%async_computation.3 | async-start | bytes 8650752 | tf_op jit(solution)/shard_map/reduce_scatter | solution.py:19
  60.7 4.3 %copy-start.3 = (s32[1,1,64]{2,1,0:T(1,128)S(1)}, s32[1,1,64]{2,1,0:T(1,128)}, u32[]{:S(2)}) copy-start(s32[1,1,64]{2,1,0:T(1,128)} %param.9) | copy-start | bytes 772
  78.8 102.3 %copy-start.2 = (bf16[128,256]{1,0:T(8,128)(2,1)S(1)}, bf16[128,256]{1,0:T(8,128)(2,1)}, u32[]{:S(2)}) copy-start(bf16[128,256]{1,0:T(8,128)(2,1)} %param.12) | copy-start | bytes 196612
  78.8 102.3 %copy-start.4 = (f32[256]{0:T(256)S(1)}, f32[256]{0:T(256)}, u32[]{:S(2)}) copy-start(f32[256]{0:T(256)} %param.13) | copy-start | bytes 3076
  78.8 142.8 %all-gather.5.cloned.1.call-start = ((), (), s32[]{:S(2)}) async-start(), calls=%async_computation.4 | async-start | bytes 2359296 | tf_op jit(solution)/shard_map/all_gather | solution.py:11
  183.0 210.5 %reduce-scatter.5.cloned.1.call-start = ((), (), s32[]{:S(2)}) async-start(), calls=%async_computation.5 | async-start | bytes 17301504 | tf_op jit(solution)/shard_map/reduce_scatter | solution.py:19
  269.4 124.1 %copy-start.1 = (bf16[256,256]{1,0:T(8,128)(2,1)S(1)}, bf16[256,256]{1,0:T(8,128)(2,1)}, u32[]{:S(2)}) copy-start(bf16[256,256]{1,0:T(8,128)(2,1)} %param.14) | copy-start | bytes 393220
  269.4 124.1 %copy-start.5 = (f32[256]{0:T(256)S(1)}, f32[256]{0:T(256)}, u32[]{:S(2)}) copy-start(f32[256]{0:T(256)} %param.15) | copy-start | bytes 3076
Sparse Core Ops, SparseCore 0:
  9.1 37.4 all-gather.2
  78.9 102.1 reduce-scatter.2
  183.1 38.4 all-gather.4
  269.5 123.9 reduce-scatter.4
where the time goes:
time: 403 us; the launch traced here: 402 us
  waiting for transfers between devices  304 us (75%)
  local copies, waits for them, and re-layouts  34.5 us (9%)
  other arithmetic  34.2 us (8%)
  matrix products  15.7 us (4%)
  between operations  13.1 us (3%)
    reduce_scatter x2, waiting for transfers between devices, aggregate(): mine = lax.psum_scatter(flat_sum, 'col', scatter_dimension=0, tiled=True)  226 us
    all_gather x2, waiting for transfers between devices, aggregate(): gathered = lax.all_gather(node_feats, 'row', axis=0, tiled=True)  77.2 us
    scatter-add x2, other arithmetic, aggregate(): jax.ops.segment_sum(products, local_rows, num_segments=group_blocks)  33.5 us
    dot_general x2, local copies, waits for them, and re-layouts, aggregate(): jnp.einsum('eij,ejf->eif', values, tiles, preferred_element_type=jnp.floa...  14.6 us
    broadcast_in_dim x2, local copies, waits for them, and re-layouts, aggregate(): jax.ops.segment_sum(products, local_rows, num_segments=group_blocks)  12.1 us
    dot_general x2, matrix products, aggregate(): jnp.einsum('eij,ejf->eif', values, tiles, preferred_element_type=jnp.floa...  11.9 us
  transfers between devices with their start and end apart: 4, of which 4 were waited for; matrix products, arithmetic and copies ran while one was open for 0% of the time, Pallas kernels for 0%

commit v1 on v0

v1 whole, which is shorter than its diff:
```python
import functools

import jax
import jax.numpy as jnp
from jax import lax
from jax.experimental import pallas as pl
from jax.experimental.pallas import tpu as pltpu
from jax.sharding import PartitionSpec as P

MESH = pl.DeviceIdType.MESH
BF = jnp.bfloat16
F32 = jnp.float32
BS = 128
NNZ = 64
RING = 8
UNITS = 12


def loop(n, body):
    lax.fori_loop(0, n, lambda i, carry: (body(i), carry)[1], 0)


def kernel(
    feat, rows, cols, vals, w1_in, b1_in, w2_in, b2_in, out,
    v, x, a, h, s, agg, w1, b1, w2, b2, rows_v, cols_v, idx_v, idx,
    sib_out, sib_in, q, comb, t1, r1, f, n12, n3, t2, r2,
    rs_send, rs_recv, ag_send, ag_recv, local_sem,
):
    row, col = lax.axis_index("row"), lax.axis_index("col")
    core, cx, cy = lax.rem(col, 2), lax.rem(col // 2, 4), col // 8

    def at(dz=0, dy=0, dx=0, other=False):
        yy, xx = lax.rem(cy + dy + 4, 4), lax.rem(cx + dx + 4, 4)
        kk = 1 - core if other else core
        return (lax.rem(row + dz + RING, RING), (yy * 4 + xx) * 2 + kk)

    up, down, sibling = at(dz=1), at(dz=-1), at(other=True)
    ways = (
        (at(dx=1), at(dx=-1), at(dy=1), at(dy=-1)),
        (at(dy=1), at(dy=-1), at(dx=1), at(dx=-1)),
    )
    barrier = pltpu.get_barrier_semaphore()
    for device in (up, down, sibling) + ways[0]:
        pl.semaphore_signal(barrier, inc=1, device_id=device, device_id_type=MESH)

    loads = []
    for i, (src, dst) in enumerate((
        (rows, rows_v), (cols, cols_v), (feat, x.at[0]), (vals, v), (w1_in, w1), (b1_in, b1), (w2_in, w2), (b2_in, b2),
    )):
        loads.append(pltpu.make_async_copy(src, dst, local_sem.at[i]))
        loads[-1].start()

    loads[0].wait()
    loads[1].wait()
    wide = jnp.broadcast_to(rows_v[...], (NNZ, NNZ))
    sub = lax.broadcasted_iota(jnp.int32, (NNZ, NNZ), 0)
    lane = lax.broadcasted_iota(jnp.int32, (NNZ, NNZ), 1)
    tall = jnp.sum(jnp.where(sub == lane, wide, 0), axis=1, keepdims=True)
    before = jnp.max(jnp.where((tall == wide) & (sub < lane), sub, -1), axis=0, keepdims=True)
    sub = lax.broadcasted_iota(jnp.int32, (NNZ, BS), 0)
    lane = lax.broadcasted_iota(jnp.int32, (NNZ, BS), 1)
    last = jnp.max(jnp.where(tall == lane, sub, -1), axis=0, keepdims=True)
    held = cols_v[...]
    slot = (((held >> 2) - row + RING) & (RING - 1)) * 4 + (held & 3)
    idx_v[...] = jnp.zeros_like(idx_v)
    idx_v[0:1, :] = jnp.where(last < 0, NNZ, last)
    idx_v[1:2, 0:NNZ] = jnp.where(before < 0, NNZ, before)
    idx_v[2:3, 0:NNZ] = slot
    to_scalars = pltpu.make_async_copy(idx_v, idx, local_sem.at[8])
    to_scalars.start()
    s[0, NNZ] = jnp.zeros((BS, BS), F32)
    s[1, NNZ] = jnp.zeros((BS, BS), F32)

    sends = []

    def send(src, dst, sems, at_sem, device):
        copy = pltpu.make_async_remote_copy(
            src_ref=src, dst_ref=dst, send_sem=sems[0].at[at_sem], recv_sem=sems[1].at[at_sem],
            device_id=device, device_id_type=MESH,
        )
        copy.start()
        sends.append(copy)
        return copy

    class Gather:
        def __init__(self, buf, part, number, even):
            self.buf, self.part, self.number = buf, part, number
            self.far = (4, 3) if even else (3, 4)
            self.flying = {}

        def hop(self, n):
            for way, device, source, target in (
                (0, up, (RING - n + 1) % RING, RING - n),
                (1, down, n - 1, n),
            ):
                if n <= self.far[way]:
                    self.flying[way, n] = send(
                        self.buf.at[source, self.part], self.buf.at[target, self.part],
                        (ag_send, ag_recv), (self.number, target - 1), device,
                    )

        def arrive(self, n):
            slots = []
            for way, target in ((0, RING - n), (1, n)):
                if n <= self.far[way]:
                    self.flying[way, n].wait_recv()
                    slots.append(target)
            if n < 4:
                self.hop(n + 1)
            return slots

    loads[2].wait()
    pl.semaphore_wait(barrier, 7)
    first = [Gather(x, pl.ds(2 * j, 2), j, j == 0) for j in range(2)]
    for g in first:
        g.hop(1)
    for n in range(1, 5):
        for g in first:
            g.arrive(n)
    for copy in loads[3:]:
        copy.wait()
    to_scalars.wait()

    def products(half, source):
        def body(i):
            for j in range(8):
                e = i * 8 + j
                held = source(idx[2, e])
                s[half, e] = jnp.dot(v[e], held, preferred_element_type=F32) + s[half, idx[1, e]]

        loop(NNZ // 8, body)

    class Unit:
        def __init__(self, number, half, t):
            self.u, self.half, self.t = number, half, t
            self.kind = t % 2
            self.plus1, self.minus1, self.plus2, self.minus2 = ways[self.kind]

        def send(self, src, dst, which, device):
            return send(src, dst, (rs_send, rs_recv), (self.u, which), device)

        def own(self, d, g, kk):
            if self.kind == 0:
                xx, yy = (cx + d) & 3, (cy + g) & 3
            else:
                yy, xx = (cy + d) & 3, (cx + g) & 3
            b = ((yy * 4 + xx) * 2 + kk) * 4 + self.t
            return s[self.half, idx[0, b]]

        def chip(self, d, g):
            return self.own(d, g, core) + sib_in[self.u, d * 4 + g].astype(F32)

        def stage0(self):
            u = self.u

            def body(i):
                for g in range(4):
                    sib_out[u, i * 4 + g] = self.own(i, g, 1 - core).astype(BF)

            loop(4, body)
            self.sib = self.send(sib_out.at[u], sib_in.at[u], 0, sibling)

        def stage1(self):
            u = self.u
            self.sib.wait_recv()

            def far(g):
                q[u, g] = self.chip(2, g).astype(BF)

            def near(i):
                q[u, 4 + i] = self.chip(1 + 2 * (i // 2), (i + 2) & 3).astype(BF)

            loop(4, far)
            self.m1 = [
                self.send(q.at[u, pl.ds(0, 2)], t1.at[u, pl.ds(0, 2)], 1, self.plus1),
                self.send(q.at[u, pl.ds(2, 2)], t1.at[u, pl.ds(2, 2)], 2, self.minus1),
            ]
            loop(4, near)
            self.m2 = [
                self.send(q.at[u, pl.ds(4, 2)], r1.at[u, 0, pl.ds(2, 2)], 3, self.plus1),
                self.send(q.at[u, pl.ds(6, 2)], r1.at[u, 1, pl.ds(0, 2)], 4, self.minus1),
            ]

        def stage2(self):
            u = self.u
            for copy in self.m1:
                copy.wait_recv()

            def body(i):
                comb[u, i] = (self.chip(1 + 2 * (i // 2), i) + t1[u, i].astype(F32)).astype(BF)

            loop(4, body)
            self.m3 = [
                self.send(comb.at[u, pl.ds(0, 2)], r1.at[u, 0, pl.ds(0, 2)], 5, self.plus1),
                self.send(comb.at[u, pl.ds(2, 2)], r1.at[u, 1, pl.ds(2, 2)], 6, self.minus1),
            ]

        def stage3(self):
            u = self.u
            for copy in self.m2 + self.m3:
                copy.wait_recv()

            def body(g):
                f[u, g] = self.chip(0, g) + (r1[u, 0, g].astype(F32) + r1[u, 1, g].astype(F32))

            loop(4, body)
            n12[u, 0] = f[u, 2, 0:64].astype(BF)
            n12[u, 1] = f[u, 2, 64:128].astype(BF)
            n12[u, 2] = f[u, 1, 64:128].astype(BF)
            n12[u, 3] = f[u, 3, 0:64].astype(BF)
            self.n1 = [
                self.send(n12.at[u, 0], t2.at[u, 0], 7, self.plus2),
                self.send(n12.at[u, 1], t2.at[u, 1], 8, self.minus2),
            ]
            self.n2 = [
                self.send(n12.at[u, 2], r2.at[u, 0, pl.ds(64, 64)], 9, self.plus2),
                self.send(n12.at[u, 3], r2.at[u, 1, pl.ds(0, 64)], 10, self.minus2),
            ]

        def stage4(self):
            u = self.u
            for copy in self.n1:
                copy.wait_recv()
            n3[u, 0] = (f[u, 1, 0:64] + t2[u, 0].astype(F32)).astype(BF)
            n3[u, 1] = (f[u, 3, 64:128] + t2[u, 1].astype(F32)).astype(BF)
            self.n3 = [
                self.send(n3.at[u, 0], r2.at[u, 0, pl.ds(0, 64)], 11, self.plus2),
                self.send(n3.at[u, 1], r2.at[u, 1, pl.ds(64, 64)], 12, self.minus2),
            ]

        def stage5(self):
            u = self.u
            for copy in self.n2 + self.n3:
                copy.wait_recv()
            return (f[u, 0] + (r2[u, 0].astype(F32) + r2[u, 1].astype(F32))).astype(BF)

    def hidden(n, t):
        made = jnp.dot(a[n, t], w1[...], preferred_element_type=F32) + b1[...]
        made = jnp.maximum(made, 0.0).astype(BF)
        h[0, n * 4 + t] = made[:, :BS]
        h[1, n * 4 + t] = made[:, BS:]

    products(0, lambda n: x[n // 4, n % 4])
    units = [Unit(t, 0, t) for t in range(4)]
    pairs = [units[0:2], units[2:4]]
    second = [Gather(a, t, 2 + t, t % 2 == 0) for t in range(4)]

    def each(pair, stage):
        for unit in pair:
            getattr(unit, stage)()

    def publish(pair):
        for unit in pair:
            a[0, unit.t] = unit.stage5()
            second[unit.t].hop(1)
        for unit in pair:
            hidden(0, unit.t)

    def arrive(n, ts):
        slots = [(t, second[t].arrive(n)) for t in ts]
        for t, filled in slots:
            for slot_at in filled:
                hidden(slot_at, t)

    each(pairs[0], "stage0")
    each(pairs[1], "stage0")
    each(pairs[0], "stage1")
    each(pairs[0], "stage2")
    each(pairs[1], "stage1")
    each(pairs[0], "stage3")
    each(pairs[1], "stage2")
    each(pairs[0], "stage4")
    each(pairs[1], "stage3")
    publish(pairs[0])
    each(pairs[1], "stage4")
    arrive(1, (0, 1))
    publish(pairs[1])
    arrive(2, (0, 1))
    arrive(1, (2, 3))
    arrive(3, (0, 1))
    arrive(2, (2, 3))
    arrive(4, (0, 1))
    arrive(3, (2, 3))
    arrive(4, (2, 3))

    units = [Unit(4 + i, i // 4, i % 4) for i in range(8)]
    pairs = [units[2 * i : 2 * i + 2] for i in range(4)]

    def finish(pair):
        for unit in pair:
            agg[unit.t, :, unit.half * BS : (unit.half + 1) * BS] = unit.stage5()

    products(0, lambda n: h[0, n])
    each(pairs[0], "stage0")
    each(pairs[1], "stage0")
    each(pairs[0], "stage1")
    each(pairs[1], "stage1")
    products(1, lambda n: h[1, n])
    each(pairs[0], "stage2")
    each(pairs[2], "stage0")
    each(pairs[1], "stage2")
    each(pairs[2], "stage1")
    each(pairs[0], "stage3")
    each(pairs[3], "stage0")
    each(pairs[2], "stage2")
    each(pairs[3], "stage1")
    each(pairs[1], "stage3")
    each(pairs[0], "stage4")
    each(pairs[3], "stage2")
    each(pairs[2], "stage3")
    each(pairs[1], "stage4")
    finish(pairs[0])
    each(pairs[3], "stage3")
    each(pairs[2], "stage4")
    finish(pairs[1])
    each(pairs[3], "stage4")
    finish(pairs[2])
    finish(pairs[3])
    for t in range(4):
        made = jnp.dot(agg[t], w2[...], preferred_element_type=F32) + b2[...]
        out[t * BS : (t + 1) * BS, :] = jnp.maximum(made, 0.0).astype(BF)
    for copy in sends:
        copy.wait_send()


def local(features, block_rows, block_cols, block_values, weight_one, bias_one, weight_two, bias_two):
    block = (BS, BS)
    return pl.pallas_call(
        kernel,
        out_shape=jax.ShapeDtypeStruct((512, 256), BF),
        in_specs=[pl.BlockSpec(memory_space=pl.ANY)] * 8,
        out_specs=pl.BlockSpec(memory_space=pltpu.VMEM),
        scratch_shapes=[
            pltpu.VMEM((NNZ, *block), BF),
            pltpu.VMEM((RING, 4, *block), BF),
            pltpu.VMEM((RING, 4, *block), BF),
            pltpu.VMEM((2, RING * 4, *block), BF),
            pltpu.VMEM((2, NNZ + 1, *block), F32),
            pltpu.VMEM((4, BS, 2 * BS), BF),
            pltpu.VMEM((128, 256), BF),
            pltpu.VMEM((1, 256), F32),
            pltpu.VMEM((256, 256), BF),
            pltpu.VMEM((1, 256), F32),
            pltpu.VMEM((1, NNZ), jnp.int32),
            pltpu.VMEM((1, NNZ), jnp.int32),
            pltpu.VMEM((8, BS), jnp.int32),
            pltpu.SMEM((8, BS), jnp.int32),
            pltpu.VMEM((UNITS, 16, *block), BF),
            pltpu.VMEM((UNITS, 16, *block), BF),
            pltpu.VMEM((UNITS, 8, *block), BF),
            pltpu.VMEM((UNITS, 4, *block), BF),
            pltpu.VMEM((UNITS, 4, *block), BF),
            pltpu.VMEM((UNITS, 2, 4, *block), BF),
            pltpu.VMEM((UNITS, 4, *block), F32),
            pltpu.VMEM((UNITS, 4, 64, BS), BF),
            pltpu.VMEM((UNITS, 2, 64, BS), BF),
            pltpu.VMEM((UNITS, 2, 64, BS), BF),
            pltpu.VMEM((UNITS, 2, *block), BF),
            pltpu.SemaphoreType.DMA((UNITS, 13)),
            pltpu.SemaphoreType.DMA((UNITS, 13)),
            pltpu.SemaphoreType.DMA((6, 7)),
            pltpu.SemaphoreType.DMA((6, 7)),
            pltpu.SemaphoreType.DMA((9,)),
        ],
        compiler_params=pltpu.CompilerParams(
            collective_id=1, has_side_effects=True, vmem_limit_bytes=56 * 2**20
        ),
        name="two_layers",
    )(
        features.reshape(4, *block),
        block_rows.reshape(1, NNZ),
        block_cols.reshape(1, NNZ),
        block_values.reshape(NNZ, *block),
        weight_one,
        bias_one.reshape(1, -1),
        weight_two,
        bias_two.reshape(1, -1),
    )


def solution(mesh):
    placed = (
        P(("row", "col"), None),
        P("row", "col", None),
        P("row", "col", None),
        P("row", "col", None, None, None),
        P(),
        P(),
        P(),
        P(),
    )
    return jax.shard_map(
        local, mesh=mesh, in_specs=placed, out_specs=P(("row", "col"), None), check_vma=False
    )
```

time: 403 us -> 101 us (0.25)
  waiting for transfers between devices: 304 us -> 0 us
  Pallas kernels: 0 us -> 99.5 us
  other arithmetic: 34.2 us -> 0 us
  local copies, waits for them, and re-layouts: 34.5 us -> 1.67 us
  matrix products: 15.7 us -> 0 us
  between operations: 13.1 us -> 0.01 us
    reduce_scatter x2 -> x0, waiting for transfers between devices: 226 us -> none  [aggregate(): mine = lax.psum_scatter(flat_sum, 'col', scatter_dimension=0, tiled=True)]
    pallas_call x0 -> x1, Pallas kernels: none -> 99.5 us  [local(): pl.pallas_call(kernel, out_shape=jax.ShapeDtypeStruct((512, 256), BF), in...]
    all_gather x2 -> x0, waiting for transfers between devices: 77.2 us -> none  [aggregate(): gathered = lax.all_gather(node_feats, 'row', axis=0, tiled=True)]
    scatter-add x2 -> x0, other arithmetic: 33.5 us -> none  [aggregate(): jax.ops.segment_sum(products, local_rows, num_segments=group_blocks)]
    dot_general x4 -> x0, matrix products: 15.7 us -> none  [the longest x2 11.9 us: aggregate(): jnp.einsum('eij,ejf->eif', values, tiles, preferred_element_type=jnp.floa...]
    dot_general x2 -> x0, local copies, waits for them, and re-layouts: 14.6 us -> none  [aggregate(): jnp.einsum('eij,ejf->eif', values, tiles, preferred_element_type=jnp.floa...]
    broadcast_in_dim x2 -> x0, local copies, waits for them, and re-layouts: 12.1 us -> none  [aggregate(): jax.ops.segment_sum(products, local_rows, num_segments=group_blocks)]
    gather x2 -> x0, local copies, waits for them, and re-layouts: 7.72 us -> none  [aggregate(): tiles = blocks[local_cols]]
  transfers between devices with their start and end apart: 4 -> 0, of which waited for: 4 -> 0; matrix products, arithmetic and copies ran while one was open for 0% -> 0% of each run, Pallas kernels for 0% -> 0%
where the time goes in v1:
time: 101 us
  Pallas kernels  99.5 us (99%)
  local copies, waits for them, and re-layouts  1.67 us (2%)
    pallas_call x1, Pallas kernels, local(): pl.pallas_call(kernel, out_shape=jax.ShapeDtypeStruct((512, 256), BF), in...  99.5 us

profile of v1, /device:TPU:1, one launch (start us, length us, event | category | flops | bytes accessed | tf_op | source)
XLA Modules:
  0.0 101.2 jit_solution(10982621962004888897)
XLA Ops:
  0.0 99.5 %two_layers.1 = bf16[512,256]{1,0:T(8,128)(2,1)} custom-call(bf16[4,128,128]{2,1,0:T(8,128)(2,1)} %bitcast.7, s32[1,64]{1,0:T(1,128)} %bitcast.10, s32[1,64]{1,0:T(1,128)} %bitcast.11, bf16[64,128,128]{2,1,0:T(8,128)(2,1)} %bitcast.6, bf16[128,256]{1,0:T(8,128)(2,1)} %w1_in.1, f32[1,256]{1,0:T(1,128)} %bitcast.8, bf16[256,256]{1,0:T(8,128)(2,1)} %w2_in.1, ...), custom_call_target="tpu_custom_call" | custom-call | tf_op jit(solution)/shard_map/two_layers/pallas_call | solution.py:328
  99.5 1.7 %copy.10 = bf16[512,256]{1,0:T(8,128)(2,1)} copy(bf16[512,256]{1,0:T(8,128)(2,1)} %two_layers.1) | data formatting | bytes 524288

commit v2 on v1

v2 whole, which is shorter than its diff:
```python
import functools

import jax
import jax.numpy as jnp
from jax import lax
from jax.experimental import pallas as pl
from jax.experimental.pallas import tpu as pltpu
from jax.sharding import PartitionSpec as P

MESH = pl.DeviceIdType.MESH
BF = jnp.bfloat16
F32 = jnp.float32
BS = 128
NNZ = 64
RING = 8
UNITS = 12


def loop(n, body):
    lax.fori_loop(0, n, lambda i, carry: (body(i), carry)[1], 0)


def kernel(
    feat, rows, cols, vals, w1_in, b1_in, w2_in, b2_in, out,
    v, x, a, h, s, agg, w1, b1, w2, b2, rows_v, cols_v, idx_v, idx,
    sib_out, sib_in, q, comb, t1, r1, f, fb, r2, out_v,
    rs_send, rs_recv, ag_send, ag_recv, local_sem, out_sem,
):
    row, col = lax.axis_index("row"), lax.axis_index("col")
    core, cx, cy = lax.rem(col, 2), lax.rem(col // 2, 4), col // 8

    def at(dz=0, dy=0, dx=0, other=False):
        yy, xx = lax.rem(cy + dy + 4, 4), lax.rem(cx + dx + 4, 4)
        kk = 1 - core if other else core
        return (lax.rem(row + dz + RING, RING), (yy * 4 + xx) * 2 + kk)

    sibling = at(other=True)
    along_z = {step: at(dz=step) for step in (1, -1, 2, -2)}
    along_x = {step: at(dx=step) for step in (1, 2, -1)}
    along_y = {step: at(dy=step) for step in (1, 2, -1)}
    ways = ((along_x, along_y), (along_y, along_x))
    barrier = pltpu.get_barrier_semaphore()
    peers = [sibling, *along_z.values(), *along_x.values(), *along_y.values()]
    for device in peers:
        pl.semaphore_signal(barrier, inc=1, device_id=device, device_id_type=MESH)

    loads = []
    for i, (src, dst) in enumerate((
        (feat, x.at[0]), (rows, rows_v), (cols, cols_v), (vals, v), (w1_in, w1), (b1_in, b1), (w2_in, w2), (b2_in, b2),
    )):
        loads.append(pltpu.make_async_copy(src, dst, local_sem.at[i]))
        loads[-1].start()

    sends = []

    def send(src, dst, sems, at_sem, device):
        copy = pltpu.make_async_remote_copy(
            src_ref=src, dst_ref=dst, send_sem=sems[0].at[at_sem], recv_sem=sems[1].at[at_sem],
            device_id=device, device_id_type=MESH,
        )
        copy.start()
        sends.append(copy)
        return copy

    class Gather:
        def __init__(self, buf, part, number, plan):
            self.buf, self.part, self.number, self.plan = buf, part, number, plan
            self.flying = {}

        def start(self, n, source):
            for slot_at, step in self.plan[n]:
                if slot_at == source:
                    target = (slot_at - step) % RING
                    self.flying[target] = send(
                        self.buf.at[slot_at, self.part], self.buf.at[target, self.part],
                        (ag_send, ag_recv), (self.number, target - 1), along_z[step],
                    )

        def arrive(self, n):
            filled = [(slot_at - step) % RING for slot_at, step in self.plan[n]]
            for target in filled:
                self.flying[target].wait_recv()
                if n + 1 < len(self.plan):
                    self.start(n + 1, target)
            return filled

    ring = (
        (((0, 1), (0, -1)), ((7, 1), (1, -1)), ((6, 1), (2, -1)), ((5, 1),)),
        (((0, 1), (0, -1)), ((7, 1), (1, -1)), ((6, 1), (2, -1)), ((3, -1),)),
    )
    three = (
        (((0, 1), (0, -1)), ((7, 1), (1, -1)), ((6, 2), (6, 1), (2, -1))),
        (((0, 1), (0, -1)), ((7, 1), (1, -1)), ((2, -2), (6, 1), (2, -1))),
    )
    two = (
        (((0, 2), (0, -2), (0, 1), (0, -1)), ((6, 2), (6, 1), (2, -1))),
        (((0, 2), (0, -2), (0, 1), (0, -1)), ((2, -2), (6, 1), (2, -1))),
    )

    loads[0].wait()
    pl.semaphore_wait(barrier, len(peers))
    first = [Gather(x, t, t, three[t % 2]) for t in range(4)]
    for g in first:
        g.start(0, 0)
    loads[1].wait()
    loads[2].wait()
    wide = jnp.broadcast_to(rows_v[...], (NNZ, NNZ))
    sub = lax.broadcasted_iota(jnp.int32, (NNZ, NNZ), 0)
    lane = lax.broadcasted_iota(jnp.int32, (NNZ, NNZ), 1)
    tall = jnp.sum(jnp.where(sub == lane, wide, 0), axis=1, keepdims=True)
    before = jnp.max(jnp.where((tall == wide) & (sub < lane), sub, -1), axis=0, keepdims=True)
    sub = lax.broadcasted_iota(jnp.int32, (NNZ, BS), 0)
    lane = lax.broadcasted_iota(jnp.int32, (NNZ, BS), 1)
    last = jnp.max(jnp.where(tall == lane, sub, -1), axis=0, keepdims=True)
    held = cols_v[...]
    slot = (((held >> 2) - row + RING) & (RING - 1)) * 4 + (held & 3)
    idx_v[...] = jnp.zeros_like(idx_v)
    idx_v[0:1, :] = jnp.where(last < 0, NNZ, last)
    idx_v[1:2, 0:NNZ] = jnp.where(before < 0, NNZ, before)
    idx_v[2:3, 0:NNZ] = slot
    to_scalars = pltpu.make_async_copy(idx_v, idx, local_sem.at[8])
    to_scalars.start()
    s[0, NNZ] = jnp.zeros((BS, BS), F32)
    s[1, NNZ] = jnp.zeros((BS, BS), F32)

    for n in range(len(three[0])):
        for g in first:
            g.arrive(n)
    for copy in loads[3:]:
        copy.wait()
    to_scalars.wait()

    def products(half, source):
        def body(i):
            for j in range(8):
                e = i * 8 + j
                held = source(idx[2, e])
                s[half, e] = jnp.dot(v[e], held, preferred_element_type=F32) + s[half, idx[1, e]]

        loop(NNZ // 8, body)

    class Unit:
        def __init__(self, number, half, t):
            self.u, self.half, self.t = number, half, t
            self.kind = t % 2
            self.way1, self.way2 = ways[self.kind]

        def send(self, src, dst, which, device):
            return send(src, dst, (rs_send, rs_recv), (self.u, which), device)

        def own(self, d, g, kk):
            if self.kind == 0:
                xx, yy = (cx + d) & 3, (cy + g) & 3
            else:
                yy, xx = (cy + d) & 3, (cx + g) & 3
            b = ((yy * 4 + xx) * 2 + kk) * 4 + self.t
            return s[self.half, idx[0, b]]

        def chip(self, d, e, g):
            return self.own(d, g, core) + sib_in[self.u, e * 4 + g].astype(F32)

        def stage0(self):
            u = self.u
            self.sib = []
            for which, at_e, d, step, n in ((0, 0, 2, 0, 1), (1, 1, 1, 2, 2), (2, 3, 0, 0, 1)):

                def body(i):
                    for g in range(4):
                        sib_out[u, at_e * 4 + i * 4 + g] = self.own(d + step * i, g, 1 - core).astype(BF)

                loop(n, body)
                part = pl.ds(at_e * 4, n * 4)
                self.sib.append(self.send(sib_out.at[u, part], sib_in.at[u, part], which, sibling))

        def far(self):
            u = self.u
            self.sib[0].wait_recv()

            def body(g):
                q[u, g] = self.chip(2, 0, g).astype(BF)

            loop(4, body)
            self.m1 = [
                self.send(q.at[u, pl.ds(0, 2)], t1.at[u, pl.ds(0, 2)], 3, self.way1[1]),
                self.send(q.at[u, pl.ds(2, 2)], t1.at[u, pl.ds(2, 2)], 4, self.way1[-1]),
            ]

        def near(self):
            u = self.u
            self.sib[1].wait_recv()

            def body(i):
                q[u, 4 + i] = self.chip(1 + 2 * (i // 2), 1 + i // 2, (i + 2) & 3).astype(BF)

            loop(4, body)
            self.m2 = [
                self.send(q.at[u, pl.ds(4, 2)], r1.at[u, 0, pl.ds(2, 2)], 5, self.way1[1]),
                self.send(q.at[u, pl.ds(6, 2)], r1.at[u, 1, pl.ds(0, 2)], 6, self.way1[-1]),
            ]

        def passed(self):
            u = self.u
            for copy in self.m1:
                copy.wait_recv()

            def body(i):
                held = self.chip(1 + 2 * (i // 2), 1 + i // 2, i)
                comb[u, i] = (held + t1[u, i].astype(F32)).astype(BF)

            loop(4, body)
            self.m3 = [
                self.send(comb.at[u, pl.ds(0, 2)], r1.at[u, 0, pl.ds(0, 2)], 7, self.way1[1]),
                self.send(comb.at[u, pl.ds(2, 2)], r1.at[u, 1, pl.ds(2, 2)], 8, self.way1[-1]),
            ]

        def second(self):
            u = self.u
            self.sib[2].wait_recv()
            for copy in self.m2 + self.m3:
                copy.wait_recv()
            self.n = []
            for g in (2, 1, 3, 0):
                held = self.chip(0, 3, g) + (r1[u, 0, g].astype(F32) + r1[u, 1, g].astype(F32))
                if g == 0:
                    f[u] = held
                else:
                    fb[u, g - 1] = held.astype(BF)
                    step = -1 if g == 3 else g
                    self.n.append(self.send(fb.at[u, g - 1], r2.at[u, g - 1], 8 + g, self.way2[step]))

        def total(self):
            u = self.u
            for copy in self.n:
                copy.wait_recv()
            return (f[u] + r2[u, 0].astype(F32) + (r2[u, 1].astype(F32) + r2[u, 2].astype(F32))).astype(BF)

    def hidden(n, t):
        made = jnp.dot(a[n, t], w1[...], preferred_element_type=F32) + b1[...]
        made = jnp.maximum(made, 0.0).astype(BF)
        h[0, n * 4 + t] = made[:, :BS]
        h[1, n * 4 + t] = made[:, BS:]

    products(0, lambda n: x[n // 4, n % 4])
    units = [Unit(t, 0, t) for t in range(4)]
    pairs = [units[0:2], units[2:4]]
    second = [Gather(a, t, 4 + t, (three, three)[t // 2][t % 2]) for t in range(4)]

    def each(pair, stage):
        for unit in pair:
            getattr(unit, stage)()

    def publish(pair):
        for unit in pair:
            a[0, unit.t] = unit.total()
            second[unit.t].start(0, 0)
        for unit in pair:
            hidden(0, unit.t)

    def arrive(n, ts):
        slots = [(t, second[t].arrive(n)) for t in ts if n < len(second[t].plan)]
        for t, filled in slots:
            for slot_at in filled:
                hidden(slot_at, t)

    each(units, "stage0")
    each(units, "far")
    each(pairs[0], "near")
    each(pairs[0], "passed")
    each(pairs[1], "near")
    each(pairs[1], "passed")
    each(pairs[0], "second")
    each(pairs[1], "second")
    publish(pairs[0])
    publish(pairs[1])
    for n in range(4):
        arrive(n, (0, 1))
        arrive(n, (2, 3))

    units = [Unit(4 + i, i // 4, i % 4) for i in range(8)]
    pairs = [units[2 * i : 2 * i + 2] for i in range(4)]

    def finish(pair):
        for unit in pair:
            agg[unit.t, :, unit.half * BS : (unit.half + 1) * BS] = unit.total()

    products(0, lambda n: h[0, n])
    each(pairs[0] + pairs[1], "stage0")
    each(pairs[0], "far")
    each(pairs[1], "far")
    each(pairs[0], "near")
    products(1, lambda n: h[1, n])
    each(pairs[2] + pairs[3], "stage0")
    each(pairs[0], "passed")
    each(pairs[1], "near")
    each(pairs[2], "far")
    each(pairs[1], "passed")
    each(pairs[0], "second")
    each(pairs[2], "near")
    each(pairs[3], "far")
    each(pairs[2], "passed")
    each(pairs[1], "second")
    each(pairs[3], "near")
    each(pairs[3], "passed")
    finish(pairs[0])
    each(pairs[2], "second")
    finish(pairs[1])
    each(pairs[3], "second")
    written = []

    def put(t):
        made = jnp.dot(agg[t], w2[...], preferred_element_type=F32) + b2[...]
        out_v[t] = jnp.maximum(made, 0.0).astype(BF)
        written.append(pltpu.make_async_copy(out_v.at[t], out.at[t], out_sem.at[t]))
        written[-1].start()

    finish(pairs[2])
    put(0)
    put(1)
    finish(pairs[3])
    put(2)
    put(3)
    for copy in sends:
        copy.wait_send()
    for copy in written:
        copy.wait()


def local(features, block_rows, block_cols, block_values, weight_one, bias_one, weight_two, bias_two):
    block = (BS, BS)
    return pl.pallas_call(
        kernel,
        out_shape=jax.ShapeDtypeStruct((4, BS, 2 * BS), BF),
        in_specs=[pl.BlockSpec(memory_space=pl.ANY)] * 8,
        out_specs=pl.BlockSpec(memory_space=pl.ANY),
        scratch_shapes=[
            pltpu.VMEM((NNZ, *block), BF),
            pltpu.VMEM((RING, 4, *block), BF),
            pltpu.VMEM((RING, 4, *block), BF),
            pltpu.VMEM((2, RING * 4, *block), BF),
            pltpu.VMEM((2, NNZ + 1, *block), F32),
            pltpu.VMEM((4, BS, 2 * BS), BF),
            pltpu.VMEM((128, 256), BF),
            pltpu.VMEM((1, 256), F32),
            pltpu.VMEM((256, 256), BF),
            pltpu.VMEM((1, 256), F32),
            pltpu.VMEM((1, NNZ), jnp.int32),
            pltpu.VMEM((1, NNZ), jnp.int32),
            pltpu.VMEM((8, BS), jnp.int32),
            pltpu.SMEM((8, BS), jnp.int32),
            pltpu.VMEM((UNITS, 16, *block), BF),
            pltpu.VMEM((UNITS, 16, *block), BF),
            pltpu.VMEM((UNITS, 8, *block), BF),
            pltpu.VMEM((UNITS, 4, *block), BF),
            pltpu.VMEM((UNITS, 4, *block), BF),
            pltpu.VMEM((UNITS, 2, 4, *block), BF),
            pltpu.VMEM((UNITS, *block), F32),
            pltpu.VMEM((UNITS, 3, *block), BF),
            pltpu.VMEM((UNITS, 3, *block), BF),
            pltpu.VMEM((4, BS, 2 * BS), BF),
            pltpu.SemaphoreType.DMA((UNITS, 12)),
            pltpu.SemaphoreType.DMA((UNITS, 12)),
            pltpu.SemaphoreType.DMA((8, 7)),
            pltpu.SemaphoreType.DMA((8, 7)),
            pltpu.SemaphoreType.DMA((9,)),
            pltpu.SemaphoreType.DMA((4,)),
        ],
        compiler_params=pltpu.CompilerParams(
            collective_id=1, has_side_effects=True, vmem_limit_bytes=56 * 2**20
        ),
        name="two_layers",
    )(
        features.reshape(4, *block),
        block_rows.reshape(1, NNZ),
        block_cols.reshape(1, NNZ),
        block_values.reshape(NNZ, *block),
        weight_one,
        bias_one.reshape(1, -1),
        weight_two,
        bias_two.reshape(1, -1),
    ).reshape(512, 256)


def solution(mesh):
    placed = (
        P(("row", "col"), None),
        P("row", "col", None),
        P("row", "col", None),
        P("row", "col", None, None, None),
        P(),
        P(),
        P(),
        P(),
    )
    return jax.shard_map(
        local, mesh=mesh, in_specs=placed, out_specs=P(("row", "col"), None), check_vma=False
    )
```

time: 101 us -> 91 us (0.901)
  Pallas kernels: 99.5 us -> 89.2 us
    pallas_call x1, Pallas kernels: 99.5 us -> 89.2 us  [local(): pl.pallas_call(kernel, out_shape=jax.ShapeDtypeStruct((4, BS, 2 * BS), BF...]
where the time goes in v2:
time: 91 us; the launch traced here: 90.9 us
  Pallas kernels  89.2 us (98%)
  local copies, waits for them, and re-layouts  1.67 us (2%)
    pallas_call x1, Pallas kernels, local(): pl.pallas_call(kernel, out_shape=jax.ShapeDtypeStruct((4, BS, 2 * BS), BF...  89.2 us

profile of v2, /device:TPU:1, one launch (start us, length us, event | category | flops | bytes accessed | tf_op | source)
XLA Modules:
  0.0 90.9 jit_solution(12210341396131073075)
XLA Ops:
  0.0 89.2 %two_layers.1 = bf16[4,128,256]{2,1,0:T(8,128)(2,1)} custom-call(bf16[4,128,128]{2,1,0:T(8,128)(2,1)} %bitcast.9, s32[1,64]{1,0:T(1,128)} %bitcast.12, s32[1,64]{1,0:T(1,128)} %bitcast.13, bf16[64,128,128]{2,1,0:T(8,128)(2,1)} %bitcast.7, bf16[128,256]{1,0:T(8,128)(2,1)} %w1_in.1, f32[1,256]{1,0:T(1,128)} %bitcast.10, bf16[256,256]{1,0:T(8,128)(2,1)} %w2_in.1, ...), custom_call_target="tpu_custom_call" | custom-call | tf_op jit(solution)/shard_map/two_layers/pallas_call | solution.py:330
  89.2 1.7 %copy.10 = bf16[512,256]{1,0:T(8,128)(2,1)} copy(bf16[512,256]{1,0:T(8,128)(2,1)} %bitcast.8) | data formatting | bytes 524288

commit v3 on v0

v3 whole, which is shorter than its diff:
```python
import functools

import jax
import jax.numpy as jnp
from jax import lax
from jax.experimental import pallas as pl
from jax.experimental.pallas import tpu as pltpu
from jax.sharding import PartitionSpec as P

MESH = pl.DeviceIdType.MESH
BF = jnp.bfloat16
F32 = jnp.float32
BS = 128
NNZ = 64
RING = 8
PAIRS = 6
SIB, FIRST, COMB, SECOND, GATHER1, GATHER2 = range(6)
SIB_FAR, SIB_NEAR, FAR, SUMS, LAST_SUMS, TOTAL = range(6)


def loop(n, body):
    lax.fori_loop(0, n, lambda i, carry: (body(i), carry)[1], 0)


def kernel(
    feat, rows, cols, vals, w1_in, b1_in, w2_in, b2_in, out,
    v, x, a, h, s, agg, w1, b1, w2, b2, rows_v, cols_v, idx_v, idx,
    sib_out, sib_in, q, comb, t1, r1, f, fb, r2,
    sent, rs_recv, ag_recv, local_sem,
):
    row, col = lax.axis_index("row"), lax.axis_index("col")
    core, cx, cy = lax.rem(col, 2), lax.rem(col // 2, 4), col // 8

    def at(dz=0, dy=0, dx=0, other=False):
        yy, xx = lax.rem(cy + dy + 4, 4), lax.rem(cx + dx + 4, 4)
        kk = 1 - core if other else core
        return (lax.rem(row + dz + RING, RING), (yy * 4 + xx) * 2 + kk)

    sibling = at(other=True)
    along_z = {step: at(dz=step) for step in (1, -1, 2, -2)}
    along_x = {step: at(dx=step) for step in (1, 2, -1)}
    along_y = {step: at(dy=step) for step in (1, 2, -1)}
    ways = ((along_x, along_y), (along_y, along_x))
    barrier = pltpu.get_barrier_semaphore()
    peers = [sibling, *along_z.values(), *along_x.values(), *along_y.values()]
    for device in peers:
        pl.semaphore_signal(barrier, inc=1, device_id=device, device_id_type=MESH)

    loads = []
    for i, (src, dst) in enumerate((
        (feat, x.at[0]), (rows, rows_v), (cols, cols_v), (vals, v), (w1_in, w1), (b1_in, b1), (w2_in, w2), (b2_in, b2),
    )):
        loads.append(pltpu.make_async_copy(src, dst, local_sem.at[i]))
        loads[-1].start()

    def send(src, dst, kind, recv_sem, device):
        pltpu.make_async_remote_copy(
            src_ref=src, dst_ref=dst, send_sem=sent.at[kind], recv_sem=recv_sem,
            device_id=device, device_id_type=MESH,
        ).start()

    def arrived(ref, recv_sem):
        pltpu.make_async_remote_copy(
            src_ref=ref, dst_ref=ref, send_sem=sent.at[SIB], recv_sem=recv_sem,
            device_id=sibling, device_id_type=MESH,
        ).wait_recv()

    def all_sent(ref, kind):
        pltpu.make_async_remote_copy(
            src_ref=ref, dst_ref=ref, send_sem=sent.at[kind], recv_sem=rs_recv.at[0, 0],
            device_id=sibling, device_id_type=MESH,
        ).wait_send()

    def rounds(t):
        return (
            ((0, 1), (0, -1)),
            ((7, 1), (1, -1)),
            ((6, 2), (6, 1), (2, -1)) if t % 2 == 0 else ((2, -2), (2, -1), (6, 1)),
        )

    class Gather:
        def __init__(self, buf, layer, t):
            self.buf, self.kind, self.t, self.sems = buf, GATHER1 + layer, t, ag_recv.at[layer * 4 + t]

        def start(self, n, source):
            for slot_at, step in rounds(self.t)[n]:
                if slot_at == source:
                    target = (slot_at - step) % RING
                    send(self.buf.at[slot_at, self.t], self.buf.at[target, self.t], self.kind, self.sems.at[target - 1], along_z[step])

        def arrive(self, n):
            filled = [(slot_at - step) % RING for slot_at, step in rounds(self.t)[n]]
            if n == 2:
                filled.sort(key=lambda target: target == 4)
            for target in filled:
                arrived(self.buf.at[target, self.t], self.sems.at[target - 1])
                if n < 2:
                    self.start(n + 1, target)
            return filled

    loads[0].wait()
    pl.semaphore_wait(barrier, len(peers))
    first = [Gather(x, 0, t) for t in range(4)]
    for g in first:
        g.start(0, 0)
    loads[1].wait()
    loads[2].wait()
    wide = jnp.broadcast_to(rows_v[...], (NNZ, NNZ))
    sub = lax.broadcasted_iota(jnp.int32, (NNZ, NNZ), 0)
    lane = lax.broadcasted_iota(jnp.int32, (NNZ, NNZ), 1)
    tall = jnp.sum(jnp.where(sub == lane, wide, 0), axis=1, keepdims=True)
    before = jnp.max(jnp.where((tall == wide) & (sub < lane), sub, -1), axis=0, keepdims=True)
    sub = lax.broadcasted_iota(jnp.int32, (NNZ, BS), 0)
    lane = lax.broadcasted_iota(jnp.int32, (NNZ, BS), 1)
    last = jnp.max(jnp.where(tall == lane, sub, -1), axis=0, keepdims=True)
    held = cols_v[...]
    slot = (((held >> 2) - row + RING) & (RING - 1)) * 4 + (held & 3)
    idx_v[...] = jnp.zeros_like(idx_v)
    idx_v[0:1, :] = jnp.where(last < 0, NNZ, last)
    idx_v[1:2, 0:NNZ] = jnp.where(before < 0, NNZ, before)
    idx_v[2:3, 0:NNZ] = slot
    to_scalars = pltpu.make_async_copy(idx_v, idx, local_sem.at[8])
    to_scalars.start()
    s[0, NNZ] = jnp.zeros((BS, BS), F32)
    s[1, NNZ] = jnp.zeros((BS, BS), F32)

    for n in range(3):
        for g in first:
            g.arrive(n)
    for copy in loads[3:]:
        copy.wait()
    to_scalars.wait()

    def products(half, source):
        for e in range(NNZ):
            held = source(idx[2, e])
            s[half, e] = jnp.dot(v[e], held, preferred_element_type=F32) + s[half, idx[1, e]]

    class Pair:
        def __init__(self, number, half, j):
            self.p, self.half, self.j, self.sems = number, half, j, rs_recv.at[number]

        def own(self, w, d, g, kk):
            if w == 0:
                xx, yy = (cx + d) & 3, (cy + g) & 3
            else:
                yy, xx = (cy + d) & 3, (cx + g) & 3
            b = ((yy * 4 + xx) * 2 + kk) * 4 + self.j * 2 + w
            return s[self.half, idx[0, b]]

        def chip(self, w, d, e, g):
            return self.own(w, d, g, core) + sib_in[self.p, e, w, g].astype(F32)

        def to_sibling(self, e, d, step, n, sem):
            p = self.p
            for w in range(2):

                def body(i):
                    for g in range(4):
                        sib_out[p, e + i, w, g] = self.own(w, d + step * i, g, 1 - core).astype(BF)

                loop(n, body)
            part = pl.ds(e, n)
            send(sib_out.at[p, part], sib_in.at[p, part], SIB, self.sems.at[sem], sibling)

        def sib_far(self):
            self.to_sibling(0, 2, 0, 1, SIB_FAR)

        def sib_near(self):
            self.to_sibling(1, 1, 2, 2, SIB_NEAR)

        def sib_here(self):
            self.to_sibling(3, 0, 0, 1, SUMS)

        def far(self):
            p = self.p
            arrived(sib_in.at[p, 0], self.sems.at[SIB_FAR])
            for w in range(2):

                def body(g):
                    q[p, w, g] = self.chip(w, 2, 0, g).astype(BF)

                loop(4, body)
                for at_q, step in ((0, 1), (2, -1)):
                    part = pl.ds(at_q, 2)
                    send(q.at[p, w, part], t1.at[p, w, part], FIRST, self.sems.at[FAR], ways[w][0][step])

        def near(self):
            p = self.p
            arrived(sib_in.at[p, pl.ds(1, 2)], self.sems.at[SIB_NEAR])
            for w in range(2):

                def body(i):
                    q[p, w, 4 + i] = self.chip(w, 1 + 2 * (i // 2), 1 + i // 2, (i + 2) & 3).astype(BF)

                loop(4, body)
                for side, step in ((0, 1), (1, -1)):
                    send(
                        q.at[p, w, pl.ds(4 + 2 * side, 2)], r1.at[p, w, side, pl.ds(2 - 2 * side, 2)],
                        FIRST, self.sems.at[SUMS], ways[w][0][step],
                    )

        def passed(self):
            p = self.p
            arrived(t1.at[p], self.sems.at[FAR])
            for n, sem in ((0, SUMS), (1, LAST_SUMS)):
                for w in range(2):
                    for side, step in ((0, 1), (1, -1)):
                        g = 2 * side + n
                        held = self.chip(w, 1 + 2 * side, 1 + side, g)
                        comb[p, w, g] = (held + t1[p, w, g].astype(F32)).astype(BF)
                        send(comb.at[p, w, g], r1.at[p, w, side, g], COMB, self.sems.at[sem], ways[w][0][step])

        def sums(self, w, g):
            p = self.p
            return self.chip(w, 0, 3, g) + (r1[p, w, 0, g].astype(F32) + r1[p, w, 1, g].astype(F32))

        def away(self, w, g):
            p = self.p
            fb[p, w, g - 1] = self.sums(w, g).astype(BF)
            send(fb.at[p, w, g - 1], r2.at[p, w, g - 1], SECOND, self.sems.at[TOTAL], ways[w][1][-1 if g == 3 else g])

        def second(self):
            p = self.p
            arrived(sib_in.at[pl.ds(0, 5), 0, 0], self.sems.at[SUMS])
            for w in range(2):
                self.away(w, 2)
            arrived(r1.at[p, 0, 0], self.sems.at[LAST_SUMS])
            for g in (1, 3):
                for w in range(2):
                    self.away(w, g)
            for w in range(2):
                f[p, w] = self.sums(w, 0)

        def total(self):
            p = self.p
            arrived(r2.at[p], self.sems.at[TOTAL])
            return [
                (f[p, w] + r2[p, w, 0].astype(F32) + (r2[p, w, 1].astype(F32) + r2[p, w, 2].astype(F32))).astype(BF)
                for w in range(2)
            ]

    def hidden(n, t):
        made = jnp.dot(a[n, t], w1[...], preferred_element_type=F32) + b1[...]
        made = jnp.maximum(made, 0.0).astype(BF)
        h[0, n * 4 + t] = made[:, :BS]
        h[1, n * 4 + t] = made[:, BS:]

    products(0, lambda n: x[n // 4, n % 4])
    pairs = [Pair(j, 0, j) for j in range(2)]
    gathers = [Gather(a, 1, t) for t in range(4)]

    def publish(j):
        for w, block in enumerate(pairs[j].total()):
            a[0, 2 * j + w] = block
            gathers[2 * j + w].start(0, 0)
        for w in range(2):
            hidden(0, 2 * j + w)

    def arrive(n, j):
        filled = [(t, slot_at) for t in (2 * j, 2 * j + 1) for slot_at in gathers[t].arrive(n)]
        for t, slot_at in filled:
            hidden(slot_at, t)

    one, two = pairs
    one.sib_far()
    two.sib_far()
    one.sib_near()
    two.sib_near()
    one.sib_here()
    two.sib_here()
    one.far()
    two.far()
    one.near()
    one.passed()
    two.near()
    two.passed()
    one.second()
    two.second()
    publish(0)
    publish(1)
    for n in range(3):
        arrive(n, 0)
        arrive(n, 1)

    pairs = [Pair(2 + i, i // 2, i % 2) for i in range(4)]

    def finish(pair):
        for w, block in enumerate(pair.total()):
            agg[2 * pair.j + w, :, pair.half * BS : (pair.half + 1) * BS] = block

    one, two, three, four = pairs
    products(0, lambda n: h[0, n])
    one.sib_far()
    two.sib_far()
    one.sib_near()
    two.sib_near()
    one.sib_here()
    two.sib_here()
    one.far()
    two.far()
    one.near()
    products(1, lambda n: h[1, n])
    three.sib_far()
    four.sib_far()
    three.sib_near()
    four.sib_near()
    three.sib_here()
    four.sib_here()
    one.passed()
    two.near()
    three.far()
    two.passed()
    three.near()
    four.far()
    three.passed()
    four.near()
    four.passed()
    one.second()
    two.second()
    three.second()
    finish(one)
    finish(two)
    four.second()

    def put(t):
        made = jnp.dot(agg[t], w2[...], preferred_element_type=F32) + b2[...]
        out[t] = jnp.maximum(made, 0.0).astype(BF)

    finish(three)
    put(0)
    put(1)
    finish(four)
    put(2)
    put(3)
    all_sent(sib_out, SIB)
    all_sent(q, FIRST)
    all_sent(comb, COMB)
    all_sent(fb, SECOND)
    all_sent(x.at[pl.ds(1, 7)], GATHER1)
    all_sent(a.at[pl.ds(1, 7)], GATHER2)


def local(features, block_rows, block_cols, block_values, weight_one, bias_one, weight_two, bias_two):
    block = (BS, BS)
    return pl.pallas_call(
        kernel,
        out_shape=pltpu.VMEM((4, BS, 2 * BS), BF),
        in_specs=[pl.BlockSpec(memory_space=pl.ANY)] * 8,
        out_specs=pl.BlockSpec(memory_space=pltpu.VMEM),
        scratch_shapes=[
            pltpu.VMEM((NNZ, *block), BF),
            pltpu.VMEM((RING, 4, *block), BF),
            pltpu.VMEM((RING, 4, *block), BF),
            pltpu.VMEM((2, RING * 4, *block), BF),
            pltpu.VMEM((2, NNZ + 1, *block), F32),
            pltpu.VMEM((4, BS, 2 * BS), BF),
            pltpu.VMEM((128, 256), BF),
            pltpu.VMEM((1, 256), F32),
            pltpu.VMEM((256, 256), BF),
            pltpu.VMEM((1, 256), F32),
            pltpu.VMEM((1, NNZ), jnp.int32),
            pltpu.VMEM((1, NNZ), jnp.int32),
            pltpu.VMEM((8, BS), jnp.int32),
            pltpu.SMEM((8, BS), jnp.int32),
            pltpu.VMEM((PAIRS, 4, 2, 4, *block), BF),
            pltpu.VMEM((PAIRS, 4, 2, 4, *block), BF),
            pltpu.VMEM((PAIRS, 2, 8, *block), BF),
            pltpu.VMEM((PAIRS, 2, 4, *block), BF),
            pltpu.VMEM((PAIRS, 2, 4, *block), BF),
            pltpu.VMEM((PAIRS, 2, 2, 4, *block), BF),
            pltpu.VMEM((PAIRS, 2, *block), F32),
            pltpu.VMEM((PAIRS, 2, 3, *block), BF),
            pltpu.VMEM((PAIRS, 2, 3, *block), BF),
            pltpu.SemaphoreType.DMA((6,)),
            pltpu.SemaphoreType.DMA((PAIRS, 6)),
            pltpu.SemaphoreType.DMA((8, 7)),
            pltpu.SemaphoreType.DMA((9,)),
        ],
        compiler_params=pltpu.CompilerParams(
            collective_id=1, has_side_effects=True, vmem_limit_bytes=56 * 2**20
        ),
        name="two_layers",
    )(
        features.reshape(4, *block),
        block_rows.reshape(1, NNZ),
        block_cols.reshape(1, NNZ),
        block_values.reshape(NNZ, *block),
        weight_one,
        bias_one.reshape(1, -1),
        weight_two,
        bias_two.reshape(1, -1),
    ).reshape(512, 256)


def solution(mesh):
    placed = (
        P(("row", "col"), None),
        P("row", "col", None),
        P("row", "col", None),
        P("row", "col", None, None, None),
        P(),
        P(),
        P(),
        P(),
    )
    return jax.shard_map(
        local, mesh=mesh, in_specs=placed, out_specs=P(("row", "col"), None), check_vma=False
    )
```

time: 403 us -> 82.3 us (0.20)
  waiting for transfers between devices: 304 us -> 0 us
  Pallas kernels: 0 us -> 81.5 us
  other arithmetic: 34.2 us -> 0 us
  local copies, waits for them, and re-layouts: 34.5 us -> 0.71 us
  matrix products: 15.7 us -> 0 us
  between operations: 13.1 us -> 0.01 us
    reduce_scatter x2 -> x0, waiting for transfers between devices: 226 us -> none  [aggregate(): mine = lax.psum_scatter(flat_sum, 'col', scatter_dimension=0, tiled=True)]
    pallas_call x0 -> x1, Pallas kernels: none -> 81.5 us  [local(): pl.pallas_call(kernel, out_shape=pltpu.VMEM((4, BS, 2 * BS), BF), in_spec...]
    all_gather x2 -> x0, waiting for transfers between devices: 77.2 us -> none  [aggregate(): gathered = lax.all_gather(node_feats, 'row', axis=0, tiled=True)]
    scatter-add x2 -> x0, other arithmetic: 33.5 us -> none  [aggregate(): jax.ops.segment_sum(products, local_rows, num_segments=group_blocks)]
    dot_general x4 -> x0, matrix products: 15.7 us -> none  [the longest x2 11.9 us: aggregate(): jnp.einsum('eij,ejf->eif', values, tiles, preferred_element_type=jnp.floa...]
    dot_general x2 -> x0, local copies, waits for them, and re-layouts: 14.6 us -> none  [aggregate(): jnp.einsum('eij,ejf->eif', values, tiles, preferred_element_type=jnp.floa...]
    broadcast_in_dim x2 -> x0, local copies, waits for them, and re-layouts: 12.1 us -> none  [aggregate(): jax.ops.segment_sum(products, local_rows, num_segments=group_blocks)]
    gather x2 -> x0, local copies, waits for them, and re-layouts: 7.72 us -> none  [aggregate(): tiles = blocks[local_cols]]
  transfers between devices with their start and end apart: 4 -> 0, of which waited for: 4 -> 0; matrix products, arithmetic and copies ran while one was open for 0% -> 0% of each run, Pallas kernels for 0% -> 0%
where the time goes in v3:
time: 82.3 us; the launch traced here: 82.2 us
  Pallas kernels  81.5 us (99%)
    pallas_call x1, Pallas kernels, local(): pl.pallas_call(kernel, out_shape=pltpu.VMEM((4, BS, 2 * BS), BF), in_spec...  81.5 us

profile of v3, /device:TPU:1, one launch (start us, length us, event | category | flops | bytes accessed | tf_op | source)
XLA Modules:
  0.0 82.2 jit_solution(10041144979613714404)
XLA Ops:
  0.0 81.5 %two_layers.1 = bf16[4,128,256]{2,1,0:T(8,128)(2,1)S(1)} custom-call(bf16[4,128,128]{2,1,0:T(8,128)(2,1)} %bitcast.9, s32[1,64]{1,0:T(1,128)} %bitcast.12, s32[1,64]{1,0:T(1,128)} %bitcast.13, bf16[64,128,128]{2,1,0:T(8,128)(2,1)} %bitcast.8, bf16[128,256]{1,0:T(8,128)(2,1)} %w1_in.1, f32[1,256]{1,0:T(1,128)} %bitcast.10, bf16[256,256]{1,0:T(8,128)(2,1)} %w2_in.1, ...), custom_call_target="tpu_custom_call" | custom-call | tf_op jit(solution)/shard_map/two_layers/pallas_call | solution.py:346
  81.5 0.7 copy.10

commit v4 on v3

--- a/solution.py
+++ b/solution.py
@@ -15,7 +15,7 @@
 RING = 8
 PAIRS = 6
 SIB, FIRST, COMB, SECOND, GATHER1, GATHER2 = range(6)
-SIB_FAR, SIB_NEAR, FAR, SUMS, LAST_SUMS, TOTAL = range(6)
+SIB_FAR, SIB_NEAR, FAR, SUMS, LAST_SUMS, TOTAL, HALVES = range(7)
 
 
 def loop(n, body):
@@ -203,7 +203,7 @@
         def passed(self):
             p = self.p
             arrived(t1.at[p], self.sems.at[FAR])
-            for n, sem in ((0, SUMS), (1, LAST_SUMS)):
+            for n, sem in ((1, SUMS), (0, LAST_SUMS)):
                 for w in range(2):
                     for side, step in ((0, 1), (1, -1)):
                         g = 2 * side + n
@@ -223,14 +223,46 @@
         def second(self):
             p = self.p
             arrived(sib_in.at[pl.ds(0, 5), 0, 0], self.sems.at[SUMS])
-            for w in range(2):
-                self.away(w, 2)
-            arrived(r1.at[p, 0, 0], self.sems.at[LAST_SUMS])
             for g in (1, 3):
                 for w in range(2):
                     self.away(w, g)
+            arrived(r1.at[p, 0, 0], self.sems.at[LAST_SUMS])
+            for w in range(2):
+                self.away(w, 2)
             for w in range(2):
                 f[p, w] = self.sums(w, 0)
+
+        def part_way(self, src, dst, rows, sem, step):
+            send(fb.at[self.p, *src, rows], r2.at[self.p, *dst, rows], SECOND, self.sems.at[sem], ways[src[0]][1][step])
+
+        def second_halves(self):
+            p, upper, lower = self.p, pl.ds(0, 64), pl.ds(64, 64)
+            arrived(sib_in.at[pl.ds(0, 5), 0, 0], self.sems.at[SUMS])
+            arrived(r1.at[p, 0, 0], self.sems.at[LAST_SUMS])
+            for w in range(2):
+                fb[p, w, 0] = self.sums(w, 2).astype(BF)
+                self.part_way((w, 0), (w, 2), upper, HALVES, 1)
+                self.part_way((w, 0), (w, 2), lower, HALVES, -1)
+            for w in range(2):
+                fb[p, w, 1, 64:128] = self.sums(w, 1)[64:128].astype(BF)
+                self.part_way((w, 1), (w, 0), lower, TOTAL, 1)
+                fb[p, w, 1, 0:64] = self.sums(w, 3)[0:64].astype(BF)
+                self.part_way((w, 1), (w, 1), upper, TOTAL, -1)
+                f[p, w] = self.sums(w, 0)
+
+        def third(self):
+            p, upper, lower = self.p, pl.ds(0, 64), pl.ds(64, 64)
+            arrived(fb.at[p, 0, pl.ds(0, 2)], self.sems.at[HALVES])
+            for w in range(2):
+                fb[p, w, 2, 0:64] = (self.sums(w, 1)[0:64] + r2[p, w, 2, 0:64].astype(F32)).astype(BF)
+                self.part_way((w, 2), (w, 0), upper, TOTAL, 1)
+                fb[p, w, 2, 64:128] = (self.sums(w, 3)[64:128] + r2[p, w, 2, 64:128].astype(F32)).astype(BF)
+                self.part_way((w, 2), (w, 1), lower, TOTAL, -1)
+
+        def total_halves(self):
+            p = self.p
+            arrived(r1.at[p, 0, 0], self.sems.at[TOTAL])
+            return [(f[p, w] + (r2[p, w, 0].astype(F32) + r2[p, w, 1].astype(F32))).astype(BF) for w in range(2)]
 
         def total(self):
             p = self.p
@@ -286,7 +318,7 @@
     pairs = [Pair(2 + i, i // 2, i % 2) for i in range(4)]
 
     def finish(pair):
-        for w, block in enumerate(pair.total()):
+        for w, block in enumerate(pair.total() if pair is four else pair.total_halves()):
             agg[2 * pair.j + w, :, pair.half * BS : (pair.half + 1) * BS] = block
 
     one, two, three, four = pairs
@@ -316,12 +348,15 @@
     three.passed()
     four.near()
     four.passed()
-    one.second()
-    two.second()
-    three.second()
+    one.second_halves()
+    two.second_halves()
+    three.second_halves()
+    one.third()
+    two.third()
+    four.second()
+    three.third()
     finish(one)
     finish(two)
-    four.second()
 
     def put(t):
         made = jnp.dot(agg[t], w2[...], preferred_element_type=F32) + b2[...]
@@ -373,7 +408,7 @@
             pltpu.VMEM((PAIRS, 2, 3, *block), BF),
             pltpu.VMEM((PAIRS, 2, 3, *block), BF),
             pltpu.SemaphoreType.DMA((6,)),
-            pltpu.SemaphoreType.DMA((PAIRS, 6)),
+            pltpu.SemaphoreType.DMA((PAIRS, 7)),
             pltpu.SemaphoreType.DMA((8, 7)),
             pltpu.SemaphoreType.DMA((9,)),
         ],

time: 82.3 us -> 81.4 us (0.989)
  Pallas kernels: 81.5 us -> 80.6 us
    pallas_call x1, Pallas kernels: 81.5 us -> 80.6 us  [local(): pl.pallas_call(kernel, out_shape=pltpu.VMEM((4, BS, 2 * BS), BF), in_spec...]
where the time goes in v4:
time: 81.4 us; the launch traced here: 81.3 us
  Pallas kernels  80.6 us (99%)
    pallas_call x1, Pallas kernels, local(): pl.pallas_call(kernel, out_shape=pltpu.VMEM((4, BS, 2 * BS), BF), in_spec...  80.6 us

profile of v4, /device:TPU:1, one launch (start us, length us, event | category | flops | bytes accessed | tf_op | source)
XLA Modules:
  0.0 81.3 jit_solution(17700111052713895446)
XLA Ops:
  0.0 80.6 %two_layers.1 = bf16[4,128,256]{2,1,0:T(8,128)(2,1)S(1)} custom-call(bf16[4,128,128]{2,1,0:T(8,128)(2,1)} %bitcast.9, s32[1,64]{1,0:T(1,128)} %bitcast.12, s32[1,64]{1,0:T(1,128)} %bitcast.13, bf16[64,128,128]{2,1,0:T(8,128)(2,1)} %bitcast.8, bf16[128,256]{1,0:T(8,128)(2,1)} %w1_in.1, f32[1,256]{1,0:T(1,128)} %bitcast.10, bf16[256,256]{1,0:T(8,128)(2,1)} %w2_in.1, ...), custom_call_target="tpu_custom_call" | custom-call | tf_op jit(solution)/shard_map/two_layers/pallas_call | solution.py:381
  80.6 0.7 copy.10

commit v5 on v4

--- a/solution.py
+++ b/solution.py
@@ -318,7 +318,7 @@
     pairs = [Pair(2 + i, i // 2, i % 2) for i in range(4)]
 
     def finish(pair):
-        for w, block in enumerate(pair.total() if pair is four else pair.total_halves()):
+        for w, block in enumerate(pair.total() if pair in (three, four,) else pair.total_halves()):
             agg[2 * pair.j + w, :, pair.half * BS : (pair.half + 1) * BS] = block
 
     one, two, three, four = pairs
@@ -350,11 +350,10 @@
     four.passed()
     one.second_halves()
     two.second_halves()
-    three.second_halves()
+    three.second()
     one.third()
+    four.second()
     two.third()
-    four.second()
-    three.third()
     finish(one)
     finish(two)
 

time: 81.4 us -> 80.8 us (level)
  no operation moved by 1% of the time
where the time goes in v5:
time: 80.8 us; the launch traced here: 80.7 us
  Pallas kernels  80 us (99%)
    pallas_call x1, Pallas kernels, local(): pl.pallas_call(kernel, out_shape=pltpu.VMEM((4, BS, 2 * BS), BF), in_spec...  80 us

profile of v5, /device:TPU:1, one launch (start us, length us, event | category | flops | bytes accessed | tf_op | source)
XLA Modules:
  0.0 80.7 jit_solution(8654617810208866941)
XLA Ops:
  0.0 80.0 %two_layers.1 = bf16[4,128,256]{2,1,0:T(8,128)(2,1)S(1)} custom-call(bf16[4,128,128]{2,1,0:T(8,128)(2,1)} %bitcast.9, s32[1,64]{1,0:T(1,128)} %bitcast.12, s32[1,64]{1,0:T(1,128)} %bitcast.13, bf16[64,128,128]{2,1,0:T(8,128)(2,1)} %bitcast.8, bf16[128,256]{1,0:T(8,128)(2,1)} %w1_in.1, f32[1,256]{1,0:T(1,128)} %bitcast.10, bf16[256,256]{1,0:T(8,128)(2,1)} %w2_in.1, ...), custom_call_target="tpu_custom_call" | custom-call | tf_op jit(solution)/shard_map/two_layers/pallas_call | solution.py:380
  80.0 0.7 copy.10

commit v6 on v5

--- a/solution.py
+++ b/solution.py
@@ -26,7 +26,7 @@
     feat, rows, cols, vals, w1_in, b1_in, w2_in, b2_in, out,
     v, x, a, h, s, agg, w1, b1, w2, b2, rows_v, cols_v, idx_v, idx,
     sib_out, sib_in, q, comb, t1, r1, f, fb, r2,
-    sent, rs_recv, ag_recv, local_sem,
+    sent, rs_recv, ag_recv, ag_last, local_sem,
 ):
     row, col = lax.axis_index("row"), lax.axis_index("col")
     core, cx, cy = lax.rem(col, 2), lax.rem(col // 2, 4), col // 8
@@ -81,20 +81,20 @@
     class Gather:
         def __init__(self, buf, layer, t):
             self.buf, self.kind, self.t, self.sems = buf, GATHER1 + layer, t, ag_recv.at[layer * 4 + t]
+            self.last_sem = ag_last.at[0 if layer == 0 else 1 + t // 2]
 
         def start(self, n, source):
             for slot_at, step in rounds(self.t)[n]:
                 if slot_at == source:
                     target = (slot_at - step) % RING
-                    send(self.buf.at[slot_at, self.t], self.buf.at[target, self.t], self.kind, self.sems.at[target - 1], along_z[step])
+                    sem = self.last_sem if n == 2 else self.sems.at[(7, 1, 6, 2).index(target)]
+                    send(self.buf.at[slot_at, self.t], self.buf.at[target, self.t], self.kind, sem, along_z[step])
 
         def arrive(self, n):
             filled = [(slot_at - step) % RING for slot_at, step in rounds(self.t)[n]]
-            if n == 2:
-                filled.sort(key=lambda target: target == 4)
-            for target in filled:
-                arrived(self.buf.at[target, self.t], self.sems.at[target - 1])
-                if n < 2:
+            if n < 2:
+                for target in filled:
+                    arrived(self.buf.at[target, self.t], self.sems.at[(7, 1, 6, 2).index(target)])
                     self.start(n + 1, target)
             return filled
 
@@ -124,9 +124,10 @@
     s[0, NNZ] = jnp.zeros((BS, BS), F32)
     s[1, NNZ] = jnp.zeros((BS, BS), F32)
 
-    for n in range(3):
+    for n in range(2):
         for g in first:
             g.arrive(n)
+    arrived(x.at[pl.ds(3, 3)], ag_last.at[0])
     for copy in loads[3:]:
         copy.wait()
     to_scalars.wait()
@@ -290,6 +291,8 @@
             hidden(0, 2 * j + w)
 
     def arrive(n, j):
+        if n == 2:
+            arrived(r2.at[0], ag_last.at[1 + j])
         filled = [(t, slot_at) for t in (2 * j, 2 * j + 1) for slot_at in gathers[t].arrive(n)]
         for t, slot_at in filled:
             hidden(slot_at, t)
@@ -408,7 +411,8 @@
             pltpu.VMEM((PAIRS, 2, 3, *block), BF),
             pltpu.SemaphoreType.DMA((6,)),
             pltpu.SemaphoreType.DMA((PAIRS, 7)),
-            pltpu.SemaphoreType.DMA((8, 7)),
+            pltpu.SemaphoreType.DMA((8, 4)),
+            pltpu.SemaphoreType.DMA((3,)),
             pltpu.SemaphoreType.DMA((9,)),
         ],
         compiler_params=pltpu.CompilerParams(

time: 80.8 us -> 80.6 us (level)
  no operation moved by 1% of the time
where the time goes in v6:
time: 80.6 us; the launch traced here: 80.5 us
  Pallas kernels  79.8 us (99%)
    pallas_call x1, Pallas kernels, local(): pl.pallas_call(kernel, out_shape=pltpu.VMEM((4, BS, 2 * BS), BF), in_spec...  79.8 us

profile of v6, /device:TPU:1, one launch (start us, length us, event | category | flops | bytes accessed | tf_op | source)
XLA Modules:
  0.0 80.5 jit_solution(1026589266772960334)
XLA Ops:
  0.0 79.8 %two_layers.1 = bf16[4,128,256]{2,1,0:T(8,128)(2,1)S(1)} custom-call(bf16[4,128,128]{2,1,0:T(8,128)(2,1)} %bitcast.9, s32[1,64]{1,0:T(1,128)} %bitcast.12, s32[1,64]{1,0:T(1,128)} %bitcast.13, bf16[64,128,128]{2,1,0:T(8,128)(2,1)} %bitcast.8, bf16[128,256]{1,0:T(8,128)(2,1)} %w1_in.1, f32[1,256]{1,0:T(1,128)} %bitcast.10, bf16[256,256]{1,0:T(8,128)(2,1)} %w2_in.1, ...), custom_call_target="tpu_custom_call" | custom-call | tf_op jit(solution)/shard_map/two_layers/pallas_call | solution.py:383
  79.8 0.7 copy.10

commit v7 on v6

--- a/solution.py
+++ b/solution.py
@@ -338,13 +338,13 @@
     products(1, lambda n: h[1, n])
     three.sib_far()
     four.sib_far()
+    one.passed()
+    two.near()
+    three.far()
     three.sib_near()
     four.sib_near()
     three.sib_here()
     four.sib_here()
-    one.passed()
-    two.near()
-    three.far()
     two.passed()
     three.near()
     four.far()

time: 80.6 us -> 80.6 us (level)
  no operation moved by 1% of the time
where the time goes in v7:
time: 80.6 us; the launch traced here: 80.5 us
  Pallas kernels  79.8 us (99%)
    pallas_call x1, Pallas kernels, local(): pl.pallas_call(kernel, out_shape=pltpu.VMEM((4, BS, 2 * BS), BF), in_spec...  79.8 us

profile of v7, /device:TPU:1, one launch (start us, length us, event | category | flops | bytes accessed | tf_op | source)
XLA Modules:
  0.0 80.5 jit_solution(8635039392373139460)
XLA Ops:
  0.0 79.8 %two_layers.1 = bf16[4,128,256]{2,1,0:T(8,128)(2,1)S(1)} custom-call(bf16[4,128,128]{2,1,0:T(8,128)(2,1)} %bitcast.9, s32[1,64]{1,0:T(1,128)} %bitcast.12, s32[1,64]{1,0:T(1,128)} %bitcast.13, bf16[64,128,128]{2,1,0:T(8,128)(2,1)} %bitcast.8, bf16[128,256]{1,0:T(8,128)(2,1)} %w1_in.1, f32[1,256]{1,0:T(1,128)} %bitcast.10, bf16[256,256]{1,0:T(8,128)(2,1)} %w2_in.1, ...), custom_call_target="tpu_custom_call" | custom-call | tf_op jit(solution)/shard_map/two_layers/pallas_call | solution.py:383
  79.8 0.7 copy.10
